TPU v7x, 256 devices: a whole 4x4x8 slice. The times are simulated.
256 devices in a mesh: energy: 64 (over x, z_hi, y), space: 4 (over z_lo, core).
Axes of the slice: x: 4, y: 4, z: 8 (z_hi: 4, z_lo: 2; z = z_hi * 2 + z_lo), core: 2. Of those that a mesh axis runs over, the one named last changes fastest.
Arguments:
- screening: bfloat16 [64, 8, 3, 2, 128, 128], P('energy', 'space'), may hold values from -0.21875 to 0.21875
- polarization: bfloat16 [64, 8, 3, 2, 128, 128], P('energy', 'space'), may hold values from -6 to 6
- propagator: bfloat16 [64, 8, 3, 2, 128, 128], P('energy', 'space'), may hold values from -0.21875 to 0.21875
Outputs:
- dressed: bfloat16 [64, 8, 3, 2, 128, 128], P('energy', 'space')
All inputs are finite; a program needn't handle non-finite values.
Results may differ from a plain program's by a relative error of at most 0.015.
Values may be sent and summed in bfloat16 or wider, within the bound.
A program may use at most 64 MiB of HBM per device.

v0:
```python
import math

import jax
import jax.numpy as jnp
from jax import lax
from jax.sharding import PartitionSpec as P


def with_halo(x, sides, width):
    for axis, dim in sides:
        peers, length = (lax.axis_size(axis), x.shape[dim])
        up = [(i, (i + 1) % peers) for i in range(peers - 1)]
        down = [(j, i) for i, j in up]
        last = lax.slice_in_dim(x, length - width, length, axis=dim)
        leading = lax.slice_in_dim(x, 0, width, axis=dim)
        before = lax.ppermute(last, axis, up)
        after = lax.ppermute(leading, axis, down)
        x = jnp.concatenate([before, x, after], axis=dim)
    return x


def clip_edges(banded, first_row, row_total):
    row_count = banded.shape[1]
    row_index = first_row + jnp.arange(row_count, dtype=jnp.int32)
    band_index = jnp.arange(3, dtype=jnp.int32)
    dropped = (band_index[None, :] == 0) & (row_index[:, None] == 0) | (
        band_index[None, :] == 2
    ) & (row_index[:, None] == row_total - 1)
    keep_mask = jnp.where(dropped, 0.0, 1.0).astype(banded.dtype)
    return banded * keep_mask[None, :, :, None, None, None]


def complex_product(first, second, adjoint):
    first_real = first[:, :, 0]
    first_imag = first[:, :, 1]
    second_real = second[:, :, 0]
    second_imag = second[:, :, 1]
    if adjoint:
        form = "erij,erkj->erik"
    else:
        form = "erij,erjk->erik"

    def product(lhs, rhs):
        return jnp.einsum(form, lhs, rhs, preferred_element_type=jnp.float32)

    if adjoint:
        real_part = product(first_real, second_real) + product(first_imag, second_imag)
        imag_part = product(first_imag, second_real) - product(first_real, second_imag)
    else:
        real_part = product(first_real, second_real) - product(first_imag, second_imag)
        imag_part = product(first_real, second_imag) + product(first_imag, second_real)
    return jnp.stack([real_part, imag_part], axis=2)


def pick_rows(banded, start, row_count, band):
    return lax.slice_in_dim(banded, start, start + row_count, axis=1)[:, :, band]


def sandwich(outside, between):
    row_count = outside.shape[1] - 2
    products = {}
    for offset in range(-2, 3):
        summed = None
        for inner in range(-1, 2):
            if abs(offset - inner) <= 1:
                term = complex_product(
                    pick_rows(outside, 1, row_count, inner + 1),
                    pick_rows(between, 1 + inner, row_count, offset - inner + 1),
                    False,
                )
                summed = term if summed is None else summed + term
        products[offset] = summed.astype(jnp.bfloat16)
    bands = []
    for target in range(-1, 2):
        summed = None
        for offset in range(target - 1, target + 2):
            term = complex_product(
                products[offset],
                pick_rows(outside, 1 + target, row_count, offset - target + 1),
                True,
            )
            summed = term if summed is None else summed + term
        bands.append(summed)
    return jnp.stack(bands, axis=2)


def split_table(table):
    upper = table.astype(jnp.bfloat16)
    lower = (table - upper.astype(jnp.float32)).astype(jnp.bfloat16)
    return (upper, lower)


def plain_dot(lhs, rhs):
    return jnp.dot(lhs, rhs, preferred_element_type=jnp.float32)


def table_times_data(table_pair, data):
    return plain_dot(table_pair[0], data) + plain_dot(table_pair[1], data)


def table_times_float(table_pair, values):
    value_upper, value_lower = split_table(values)
    return (
        plain_dot(table_pair[0], value_upper)
        + plain_dot(table_pair[0], value_lower)
        + plain_dot(table_pair[1], value_upper)
    )


def convolve(propa_owned, screen_owned, factor):
    energy_count = propa_owned.shape[0]
    owned_shape = propa_owned[:, :, :, 0].shape
    freq_index = jnp.arange(2 * energy_count, dtype=jnp.int32)
    time_index = jnp.arange(energy_count, dtype=jnp.int32)
    phase = freq_index[:, None] * time_index[None, :] % (2 * energy_count)
    angle = phase.astype(jnp.float32) * (math.pi / energy_count)
    cosine = jnp.cos(angle)
    sine = jnp.sin(angle)
    cos_fwd = split_table(cosine)
    sin_fwd = split_table(sine)
    cos_back = split_table(cosine.T)
    sin_back = split_table(sine.T)

    def forward(banded):
        real_part = banded[:, :, :, 0].reshape(energy_count, -1)
        imag_part = banded[:, :, :, 1].reshape(energy_count, -1)
        return (
            table_times_data(cos_fwd, real_part) + table_times_data(sin_fwd, imag_part),
            table_times_data(cos_fwd, imag_part) - table_times_data(sin_fwd, real_part),
        )

    propa_real, propa_imag = forward(propa_owned)
    screen_real, screen_imag = forward(screen_owned)
    spec_real = propa_real * screen_real - propa_imag * screen_imag
    spec_imag = propa_real * screen_imag + propa_imag * screen_real
    weight = factor / (2 * energy_count)
    out_real = (
        table_times_float(cos_back, spec_real) - table_times_float(sin_back, spec_imag)
    ) * weight
    out_imag = (
        table_times_float(cos_back, spec_imag) + table_times_float(sin_back, spec_real)
    ) * weight
    return jnp.stack([out_real.reshape(owned_shape), out_imag.reshape(owned_shape)], axis=3)


def local(screening, polarization, propagator):
    row_count = screening.shape[1]
    order = screening.shape[-1]
    first_row = lax.axis_index("space") * row_count
    row_total = lax.axis_size("space") * row_count
    screen_masked = clip_edges(screening, first_row, row_total)
    polar_masked = clip_edges(polarization, first_row, row_total)
    propa_masked = clip_edges(propagator, first_row, row_total)
    rimmed = with_halo(jnp.stack([screen_masked, polar_masked]), (("space", 2),), 1)
    screen_padded = rimmed[0]
    polar_padded = rimmed[1]
    screened = sandwich(screen_padded, polar_padded).astype(jnp.bfloat16)
    screen_owned, propa_owned = (
        lax.all_to_all(screened, "energy", split_axis=4, concat_axis=0, tiled=True),
        lax.all_to_all(propa_masked, "energy", split_axis=4, concat_axis=0, tiled=True),
    )
    energy_count = screen_owned.shape[0]
    factor = (3.0 * order / energy_count) ** 0.5
    sigma_owned = convolve(propa_owned, screen_owned, factor).astype(jnp.bfloat16)
    sigma = lax.all_to_all(sigma_owned, "energy", split_axis=0, concat_axis=4, tiled=True)
    rimmed_late = with_halo(jnp.stack([propa_masked, sigma]), (("space", 2),), 1)
    propa_padded = rimmed_late[0]
    sigma_padded = rimmed_late[1]
    return sandwich(propa_padded, sigma_padded).astype(jnp.bfloat16)


def solution(mesh):
    in_specs = (
        P("energy", "space", None, None, None, None),
        P("energy", "space", None, None, None, None),
        P("energy", "space", None, None, None, None),
    )
    out_specs = P("energy", "space", None, None, None, None)
    return jax.shard_map(local, mesh=mesh, in_specs=in_specs, out_specs=out_specs, check_vma=False)
```

profile of v0, /device:TPU:1, one launch (start us, length us, event | category | flops | bytes accessed | tf_op | source)
XLA Modules:
  0.0 126.9 jit_solution(8185278999337063013)
XLA Ops:
  0.1 1.4 %fusion.85 = (bf16[1,1,2,3,2,128,128]{6,5,2,4,3,1,0:T(8,128)(2,1)S(1)}, bf16[1,1,2,3,2,128,128]{6,5,2,4,3,1,0:T(8,128)(2,1)S(1)}, bf16[1,2,3,2,128,128]{5,4,1,3,2,0:T(8,128)(2,1)S(1)}) fusion(bf16[1,2,3,2,128,128]{5,4,3,2,1,0:T(8,128)(2,1)} %param.3, bf16[2,3]{0,1:T(4,128)(2,1)S(1)} %select_convert_fusion, bf16[1,2,3,2,128,128]{5,4,3,2,1,0:T(8,128)(2,1)} %param.4, ...), kind=kLoop, calls=%fused_computation.195 | loop fusion | flops 589824 | bytes 2359308 | tf_op jit(solution)/shard_map/stack | solution.py:154
  1.6 4.9 %collective-permute-start = (bf16[2,1,1,3,2,128,128]{6,5,2,4,3,1,0:T(8,128)(2,1)S(1)}, bf16[2,1,1,3,2,128,128]{6,5,2,4,3,1,0:T(8,128)(2,1)S(1)}, u32[]{:S(2)}, u32[]{:S(2)}) collective-permute-start(bf16[2,1,1,3,2,128,128]{6,5,2,4,3,1,0:T(8,128)(2,1)S(1)} %get-tuple-element.49), channel_id=1, source_target_pairs={{0,1},{1,2},{2,3},{4,5},{5,6},{6,7},{8,9},{9,10},{10,11},{12,13},{... | collective-permute-start | bytes 1179656 | tf_op jit(solution)/shard_map/ppermute | solution.py:16
  6.5 1.9 %collective-permute-start.1 = (bf16[2,1,1,3,2,128,128]{6,5,2,4,3,1,0:T(8,128)(2,1)S(1)}, bf16[2,1,1,3,2,128,128]{6,5,2,4,3,1,0:T(8,128)(2,1)S(1)}, u32[]{:S(2)}, u32[]{:S(2)}) collective-permute-start(bf16[2,1,1,3,2,128,128]{6,5,2,4,3,1,0:T(8,128)(2,1)S(1)} %get-tuple-element.50), channel_id=1, source_target_pairs={{1,0},{2,1},{3,2},{5,4},{6,5},{7,6},{9,8},{10,9},{11,10},{13,12},{... | collective-permute-start | bytes 1179656 | tf_op jit(solution)/shard_map/ppermute | solution.py:17
  8.4 1.1 copy.19
  9.6 13.4 %all-to-all-start = ((bf16[1,2,3,2,128,128]{5,1,3,2,0,4:T(2,128)(2,1)}), bf16[1,2,3,2,128,128]{5,1,3,2,0,4:T(2,128)(2,1)S(1)}, u32[]{:S(2)}, u32[]{:S(2)}) async-start(bf16[1,2,3,2,128,128]{5,1,3,2,0,4:T(2,128)(2,1)} %copy.19), calls=%async_computation | async-start | bytes 786432 | tf_op jit(solution)/shard_map/all_to_all | solution.py:160
  36.2 1.2 copy.23
  37.3 3.1 %all-to-all-done = bf16[1,2,3,2,128,128]{5,1,3,2,0,4:T(2,128)(2,1)S(1)} async-done(((bf16[1,2,3,2,128,128]{5,1,3,2,0,4:T(2,128)(2,1)}), bf16[1,2,3,2,128,128]{5,1,3,2,0,4:T(2,128)(2,1)S(1)}, u32[]{:S(2)}, u32[]{:S(2)}) %all-to-all-start) | async-done | bytes 393248 | tf_op jit(solution)/shard_map/all_to_all | solution.py:160
  40.4 9.3 %all-to-all-start.1 = ((bf16[1,2,3,2,128,128]{5,1,3,2,0,4:T(2,128)(2,1)}), bf16[1,2,3,2,128,128]{5,1,3,2,0,4:T(2,128)(2,1)S(1)}, u32[]{:S(2)}, u32[]{:S(2)}) async-start(bf16[1,2,3,2,128,128]{5,1,3,2,0,4:T(2,128)(2,1)} %copy.23), calls=%async_computation.1 | async-start | bytes 786432 | tf_op jit(solution)/shard_map/all_to_all | solution.py:159
  50.4 1.4 %fusion.199 = f32[128,1536]{1,0:T(8,128)} fusion(bf16[64,1536]{1,0:T(8,128)(2,1)S(1)} %reshape_squeeze.13), kind=kOutput, calls=%fused_computation.450 | convolution fusion | flops 25288704 | bytes 983040 | tf_op jit(solution)/shard_map/dot_general | solution.py:94
  51.8 0.5 fusion.203
  52.3 0.5 fusion.207
  52.8 0.5 convolution_add_fusion.7
  53.3 1.3 %fusion.195 = f32[128,1536]{1,0:T(8,128)} fusion(bf16[64,1536]{1,0:T(8,128)(2,1)S(1)} %reshape_squeeze.12), kind=kOutput, calls=%fused_computation.448 | convolution fusion | flops 25288704 | bytes 983040 | tf_op jit(solution)/shard_map/dot_general | solution.py:94
  54.6 0.5 convolution_add_fusion.3
  55.1 1.4 %fusion.3 = f32[128,1536]{1,0:T(8,128)} fusion(f32[128,1536]{1,0:T(8,128)S(1)} %convolution_add_fusion.7, f32[128,1536]{1,0:T(8,128)S(1)} %copy-done, bf16[64,1536]{1,0:T(8,128)(2,1)S(1)} %reshape_squeeze.13), kind=kOutput, calls=%fused_computation.10 | convolution fusion | flops 25706496 | bytes 2555904 | tf_op jit(solution)/shard_map/dot_general | solution.py:94
  56.5 10.5 %all-to-all-done.1 = bf16[1,2,3,2,128,128]{5,1,3,2,0,4:T(2,128)(2,1)S(1)} async-done(((bf16[1,2,3,2,128,128]{5,1,3,2,0,4:T(2,128)(2,1)}), bf16[1,2,3,2,128,128]{5,1,3,2,0,4:T(2,128)(2,1)S(1)}, u32[]{:S(2)}, u32[]{:S(2)}) %all-to-all-start.1) | async-done | bytes 393248 | tf_op jit(solution)/shard_map/all_to_all | solution.py:159
  67.6 1.4 %fusion.193 = f32[128,1536]{1,0:T(8,128)} fusion(bf16[64,1536]{1,0:T(8,128)(2,1)S(1)} %reshape_squeeze.14), kind=kOutput, calls=%fused_computation.447 | convolution fusion | flops 25288704 | bytes 983040 | tf_op jit(solution)/shard_map/dot_general | solution.py:94
  69.5 0.5 fusion.201
  70.0 0.5 fusion.197
  70.5 0.5 convolution_add_fusion.1
  70.9 0.5 convolution_add_fusion.5
  71.6 0.5 fusion
  72.1 0.5 fusion.2
  72.6 0.6 copy-done.2
  73.5 0.6 multiply_add_fusion
  78.0 0.6 pad_maximum_fusion.5
  78.9 20.2 %all_to_all.51 = bf16[64,2,3,2,2,128]{5,4,1,3,2,0:T(2,128)(2,1)S(1)} all-to-all(bf16[64,2,3,2,2,128]{5,4,1,3,2,0:T(2,128)(2,1)S(1)} %copy.29), channel_id=1, replica_groups=mesh['energy'=64,'space'=4] {'energy'}, dimensions={0} | all-to-all | bytes 786432 | tf_op jit(solution)/shard_map/all_to_all | solution.py:165
  99.5 4.4 %collective-permute-start.2 = (bf16[2,1,1,3,2,128,128]{6,5,2,4,3,1,0:T(8,128)(2,1)S(1)}, bf16[2,1,1,3,2,128,128]{6,5,2,4,3,1,0:T(8,128)(2,1)S(1)}, u32[]{:S(2)}, u32[]{:S(2)}) collective-permute-start(bf16[2,1,1,3,2,128,128]{6,5,2,4,3,1,0:T(8,128)(2,1)S(1)} %get-tuple-element.29), channel_id=1, source_target_pairs={{0,1},{1,2},{2,3},{4,5},{5,6},{6,7},{8,9},{9,10},{10,11},{12,13},{... | collective-permute-start | bytes 1179656 | tf_op jit(solution)/shard_map/ppermute | solution.py:16
  103.9 2.0 %collective-permute-start.3 = (bf16[2,1,1,3,2,128,128]{6,5,2,4,3,1,0:T(8,128)(2,1)S(1)}, bf16[2,1,1,3,2,128,128]{6,5,2,4,3,1,0:T(8,128)(2,1)S(1)}, u32[]{:S(2)}, u32[]{:S(2)}) collective-permute-start(bf16[2,1,1,3,2,128,128]{6,5,2,4,3,1,0:T(8,128)(2,1)S(1)} %get-tuple-element.30), channel_id=1, source_target_pairs={{1,0},{2,1},{3,2},{5,4},{6,5},{7,6},{9,8},{10,9},{11,10},{13,12},{... | collective-permute-start | bytes 1179656 | tf_op jit(solution)/shard_map/ppermute | solution.py:17
  105.8 2.7 %collective-permute-done.2 = bf16[2,1,1,3,2,128,128]{6,5,2,4,3,1,0:T(8,128)(2,1)S(1)} collective-permute-done((bf16[2,1,1,3,2,128,128]{6,5,2,4,3,1,0:T(8,128)(2,1)S(1)}, bf16[2,1,1,3,2,128,128]{6,5,2,4,3,1,0:T(8,128)(2,1)S(1)}, u32[]{:S(2)}, u32[]{:S(2)}) %collective-permute-start.2) | collective-permute-done | bytes 393248 | tf_op jit(solution)/shard_map/ppermute | solution.py:16
  108.6 4.4 %collective-permute-done.3 = bf16[2,1,1,3,2,128,128]{6,5,2,4,3,1,0:T(8,128)(2,1)S(1)} collective-permute-done((bf16[2,1,1,3,2,128,128]{6,5,2,4,3,1,0:T(8,128)(2,1)S(1)}, bf16[2,1,1,3,2,128,128]{6,5,2,4,3,1,0:T(8,128)(2,1)S(1)}, u32[]{:S(2)}, u32[]{:S(2)}) %collective-permute-start.3) | collective-permute-done | bytes 393248 | tf_op jit(solution)/shard_map/ppermute | solution.py:17
  126.1 0.8 copy.28
  (205 shorter events, 33.1 us)
Async XLA Ops:
  1.6 21.4 %collective-permute-start = (bf16[2,1,1,3,2,128,128]{6,5,2,4,3,1,0:T(8,128)(2,1)S(1)}, bf16[2,1,1,3,2,128,128]{6,5,2,4,3,1,0:T(8,128)(2,1)S(1)}, u32[]{:S(2)}, u32[]{:S(2)}) collective-permute-start(bf16[2,1,1,3,2,128,128]{6,5,2,4,3,1,0:T(8,128)(2,1)S(1)} %get-tuple-element.49), channel_id=1, source_target_pairs={{0,1},{1,2},{2,3},{4,5},{5,6},{6,7},{8,9},{9,10},{10,11},{12,13},{... | collective-permute-start | bytes 1179656 | tf_op jit(solution)/shard_map/ppermute | solution.py:16
  6.5 16.5 %collective-permute-start.1 = (bf16[2,1,1,3,2,128,128]{6,5,2,4,3,1,0:T(8,128)(2,1)S(1)}, bf16[2,1,1,3,2,128,128]{6,5,2,4,3,1,0:T(8,128)(2,1)S(1)}, u32[]{:S(2)}, u32[]{:S(2)}) collective-permute-start(bf16[2,1,1,3,2,128,128]{6,5,2,4,3,1,0:T(8,128)(2,1)S(1)} %get-tuple-element.50), channel_id=1, source_target_pairs={{1,0},{2,1},{3,2},{5,4},{6,5},{7,6},{9,8},{10,9},{11,10},{13,12},{... | collective-permute-start | bytes 1179656 | tf_op jit(solution)/shard_map/ppermute | solution.py:17
  9.6 30.9 %all-to-all-start = ((bf16[1,2,3,2,128,128]{5,1,3,2,0,4:T(2,128)(2,1)}), bf16[1,2,3,2,128,128]{5,1,3,2,0,4:T(2,128)(2,1)S(1)}, u32[]{:S(2)}, u32[]{:S(2)}) async-start(bf16[1,2,3,2,128,128]{5,1,3,2,0,4:T(2,128)(2,1)} %copy.19), calls=%async_computation | async-start | bytes 786432 | tf_op jit(solution)/shard_map/all_to_all | solution.py:160
  40.4 26.5 %all-to-all-start.1 = ((bf16[1,2,3,2,128,128]{5,1,3,2,0,4:T(2,128)(2,1)}), bf16[1,2,3,2,128,128]{5,1,3,2,0,4:T(2,128)(2,1)S(1)}, u32[]{:S(2)}, u32[]{:S(2)}) async-start(bf16[1,2,3,2,128,128]{5,1,3,2,0,4:T(2,128)(2,1)} %copy.23), calls=%async_computation.1 | async-start | bytes 786432 | tf_op jit(solution)/shard_map/all_to_all | solution.py:159
  53.2 1.8 %copy-start = (f32[128,1536]{1,0:T(8,128)S(1)}, f32[128,1536]{1,0:T(8,128)}, u32[]{:S(2)}) copy-start(f32[128,1536]{1,0:T(8,128)} %fusion.199) | copy-start | bytes 2359300
  70.5 1.1 copy-start.1
  72.1 1.1 copy-start.2
  72.1 1.4 %copy-start.3 = (f32[128,1536]{1,0:T(8,128)S(1)}, f32[128,1536]{1,0:T(8,128)}, u32[]{:S(2)}) copy-start(f32[128,1536]{1,0:T(8,128)} %fusion.3) | copy-start | bytes 2359300
  99.5 9.1 %collective-permute-start.2 = (bf16[2,1,1,3,2,128,128]{6,5,2,4,3,1,0:T(8,128)(2,1)S(1)}, bf16[2,1,1,3,2,128,128]{6,5,2,4,3,1,0:T(8,128)(2,1)S(1)}, u32[]{:S(2)}, u32[]{:S(2)}) collective-permute-start(bf16[2,1,1,3,2,128,128]{6,5,2,4,3,1,0:T(8,128)(2,1)S(1)} %get-tuple-element.29), channel_id=1, source_target_pairs={{0,1},{1,2},{2,3},{4,5},{5,6},{6,7},{8,9},{9,10},{10,11},{12,13},{... | collective-permute-start | bytes 1179656 | tf_op jit(solution)/shard_map/ppermute | solution.py:16
  103.9 9.1 %collective-permute-start.3 = (bf16[2,1,1,3,2,128,128]{6,5,2,4,3,1,0:T(8,128)(2,1)S(1)}, bf16[2,1,1,3,2,128,128]{6,5,2,4,3,1,0:T(8,128)(2,1)S(1)}, u32[]{:S(2)}, u32[]{:S(2)}) collective-permute-start(bf16[2,1,1,3,2,128,128]{6,5,2,4,3,1,0:T(8,128)(2,1)S(1)} %get-tuple-element.30), channel_id=1, source_target_pairs={{1,0},{2,1},{3,2},{5,4},{6,5},{7,6},{9,8},{10,9},{11,10},{13,12},{... | collective-permute-start | bytes 1179656 | tf_op jit(solution)/shard_map/ppermute | solution.py:17
where the time goes:
time: 127 us
  matrix products  38.8 us (31%)
  starting transfers between devices  35.8 us (28%)
  waiting for transfers between devices  20.7 us (16%)
  blocking collectives  20.2 us (16%)
  local copies, waits for them, and re-layouts  7.44 us (6%)
  other arithmetic  3.18 us (3%)
    dot_general x144, matrix products, product(): return jnp.einsum(form, lhs, rhs, preferred_element_type=jnp.float32)  23.9 us
    all_to_all x1, blocking collectives, local(): lax.all_to_all(sigma_owned, 'energy', split_axis=0, concat_axis=4, tiled=...  20.2 us
    dot_general x28, matrix products, plain_dot(): return jnp.dot(lhs, rhs, preferred_element_type=jnp.float32)  15 us
    all_to_all x1, starting transfers between devices, local(): lax.all_to_all(propa_masked, 'energy', split_axis=4, concat_axis=0, tiled...  13.4 us
    all_to_all x1, waiting for transfers between devices, local(): lax.all_to_all(screened, 'energy', split_axis=4, concat_axis=0, tiled=True)  10.5 us
    ppermute x2, starting transfers between devices, with_halo(): before = lax.ppermute(last, axis, up)  9.31 us
    all_to_all x1, starting transfers between devices, local(): lax.all_to_all(screened, 'energy', split_axis=4, concat_axis=0, tiled=True)  9.25 us
    ppermute x2, waiting for transfers between devices, with_halo(): after = lax.ppermute(leading, axis, down)  4.4 us
  transfers between devices with their start and end apart: 6, of which 4 were waited for; matrix products, arithmetic and copies ran while one was open for 17% of the time, Pallas kernels for 0%

commit v1 on v0

v1 whole, which is shorter than its diff:
```python
import math

import jax
import jax.numpy as jnp
import ml_dtypes
import numpy as np
from jax import lax
from jax.experimental import pallas as pl
from jax.experimental.pallas import tpu as pltpu
from jax.sharding import PartitionSpec as P

MESH = pl.DeviceIdType.MESH
B = 128
NE = 64
NS = 4
HALF = NE // 2
F32 = jnp.float32
BF16 = jnp.bfloat16


def split_np(table):
    upper = table.astype(ml_dtypes.bfloat16)
    lower = (table - upper.astype(np.float64)).astype(ml_dtypes.bfloat16)
    return upper, lower


def tables(factor):
    freq = np.arange(2 * NE)
    time = np.arange(NE)
    angle = (freq[:, None] * time[None, :] % (2 * NE)) * (math.pi / NE)
    cos, sin = np.cos(angle), np.sin(angle)
    fwd = np.block([[cos, sin], [-sin, cos]])
    back = np.block([[cos.T, -sin.T], [sin.T, cos.T]]) * (factor / (2 * NE))
    fh, fl = split_np(fwd)
    bh, bl = split_np(back)
    return np.concatenate([fh, fl], 1), np.concatenate([bh, bh, bl], 1)


def dot(a, b):
    return jnp.dot(a, b, preferred_element_type=F32)


def dot_nt(a, b):
    return lax.dot_general(a, b, (((1,), (1,)), ((), ())), preferred_element_type=F32)


def wide(ref, row, band):
    return jnp.concatenate([ref[row, band, 0], ref[row, band, 1]], axis=1)


def embed(ref, row, band):
    re, im = ref[row, band, 0], ref[row, band, 1]
    return jnp.concatenate(
        [jnp.concatenate([re, im], axis=1), jnp.concatenate([-im, re], axis=1)], axis=0
    )


def sandwich_row(outer, inner, row):
    products = {}
    for offset in range(-2, 3):
        steps = [k for k in (-1, 0, 1) if abs(offset - k) <= 1]
        lhs = jnp.concatenate([wide(outer, row, k + 1) for k in steps], axis=1)
        rhs = jnp.concatenate([embed(inner, row + k, offset - k + 1) for k in steps], axis=0)
        products[offset] = dot(lhs, rhs).astype(BF16)
    bands = []
    for target in (-1, 0, 1):
        offsets = range(target - 1, target + 2)
        lhs = jnp.concatenate([products[d] for d in offsets], axis=1)
        rhs = jnp.concatenate([embed(outer, row + target, d - target + 1) for d in offsets], axis=1)
        bands.append(dot_nt(lhs, rhs))
    return bands


def pack(re, im):
    re, im = re.reshape(16, 8, B), im.reshape(16, 8, B)
    low = lax.broadcasted_iota(jnp.int32, (16, 8, B), 1) < 4
    even = jnp.where(low, re, pltpu.roll(im, 4, 1))
    odd = jnp.where(low, pltpu.roll(re, 4, 1), im)
    return jnp.stack([even, odd], axis=1).reshape(HALF, 8, B)


def unpack(packed):
    pairs = packed.reshape(16, 2, 8, B)
    even, odd = pairs[:, 0], pairs[:, 1]
    low = lax.broadcasted_iota(jnp.int32, (16, 8, B), 1) < 4
    re = jnp.where(low, even, pltpu.roll(odd, 4, 1))
    im = jnp.where(low, pltpu.roll(even, 4, 1), odd)
    return re.reshape(B, B), im.reshape(B, B)


def kernel(
    w_hbm, p_hbm, g_hbm, fwd_ref, back_ref, out_ref,
    w4, p4, g4, s4, g_send, g_recv, s_send, s_recv, c_send, c_recv, c_prev, c_next,
    g_spec, stage, load_sem, edge_send, edge_recv, swap_send, swap_recv,
):
    e = lax.axis_index("energy")
    s = lax.axis_index("space")
    barrier = pltpu.get_barrier_semaphore()
    loads = [
        pltpu.make_async_copy(src, dst.at[pl.ds(1, 2)], load_sem.at[i])
        for i, (src, dst) in enumerate(((g_hbm, g4), (w_hbm, w4), (p_hbm, p4)))
    ]
    for load in loads:
        load.start()

    def greet(i, carry):
        pl.semaphore_signal(barrier, inc=1, device_id=(lax.rem(e + i, NE), s), device_id_type=MESH)
        return carry

    @pl.when(s > 0)
    def _():
        pl.semaphore_signal(barrier, inc=1, device_id=(e, s - 1), device_id_type=MESH)

    @pl.when(s < NS - 1)
    def _():
        pl.semaphore_signal(barrier, inc=1, device_id=(e, s + 1), device_id_type=MESH)

    lax.fori_loop(1, NE, greet, 0)

    for load in loads:
        load.wait()

    @pl.when(s == 0)
    def _():
        for ref in (w4, p4, g4):
            ref[0] = jnp.zeros(ref.shape[1:], BF16)
            ref[1, 0] = jnp.zeros(ref.shape[2:], BF16)
        c_prev[...] = jnp.zeros(c_prev.shape, BF16)

    @pl.when(s == NS - 1)
    def _():
        for ref in (w4, p4, g4):
            ref[3] = jnp.zeros(ref.shape[1:], BF16)
            ref[2, 2] = jnp.zeros(ref.shape[2:], BF16)
        c_next[...] = jnp.zeros(c_next.shape, BF16)

    for c in range(3):
        for half in range(2):
            band = c if half == 0 else 2 - c
            re = g4[1 + half, band, 0].astype(F32)
            im = g4[1 + half, band, 1].astype(F32)
            g_send[c, pl.ds(half * HALF, HALF)] = pack(re, im).astype(BF16)

    pl.semaphore_wait(barrier, NE - 1 + (s > 0).astype(jnp.int32) + (s < NS - 1).astype(jnp.int32))

    def to_next(src, dst, i):
        return pltpu.make_async_remote_copy(
            src, dst, edge_send.at[i], edge_recv.at[i], device_id=(e, s + 1), device_id_type=MESH
        )

    def to_prev(src, dst, i):
        return pltpu.make_async_remote_copy(
            src, dst, edge_send.at[i], edge_recv.at[i], device_id=(e, s - 1), device_id_type=MESH
        )

    w_next, w_prev = to_next(w4.at[2], w4.at[0], 0), to_prev(w4.at[1], w4.at[3], 1)
    p_next, p_prev = to_next(p4.at[2], p4.at[0], 2), to_prev(p4.at[1], p4.at[3], 3)
    g_next, g_prev = to_next(g4.at[2], g4.at[0], 4), to_prev(g4.at[1], g4.at[3], 5)
    c_nexts = [to_next(c_recv.at[c, pl.ds(HALF, HALF)], c_prev.at[c], 6 + c) for c in range(3)]
    c_prevs = [to_prev(c_recv.at[c, pl.ds(0, HALF)], c_next.at[c], 9 + c) for c in range(3)]

    def edges(nexts, prevs, action):
        forward, backward = (prevs, nexts) if action == "wait_recv" else (nexts, prevs)

        @pl.when(s < NS - 1)
        def _():
            for copy in forward:
                getattr(copy, action)()

        @pl.when(s > 0)
        def _():
            for copy in backward:
                getattr(copy, action)()

    def swap(send, recv, slot):
        def body(i, carry):
            to = lax.rem(e + i, NE)
            pltpu.make_async_remote_copy(
                send.at[:, to], recv.at[:, e], swap_send.at[slot], swap_recv.at[slot],
                device_id=(to, s), device_id_type=MESH,
            ).start()
            return carry

        lax.fori_loop(1, NE, body, 0)
        pltpu.make_async_copy(send.at[:, e], recv.at[:, e], swap_recv.at[slot]).start()

    def wait_swap(recv, slot):
        pltpu.make_async_copy(recv, recv, swap_recv.at[slot]).wait()

    def wait_sent(send, slot):
        part = send.at[:, pl.ds(0, NE - 1)]
        pltpu.make_async_copy(part, part, swap_send.at[slot]).wait()

    edges([w_next, p_next], [w_prev, p_prev], "start")
    swap(g_send, g_recv, 0)
    edges([w_next, p_next], [w_prev, p_prev], "wait_recv")

    for half in range(2):
        bands = sandwich_row(w4, p4, 1 + half)
        for band in range(3):
            c = band if half == 0 else 2 - band
            s_send[c, pl.ds(half * HALF, HALF)] = pack(
                bands[band][:, :B], bands[band][:, B:]
            ).astype(BF16)
    swap(s_send, s_recv, 1)
    edges([g_next], [g_prev], "start")

    def spectrum(recv, c):
        stage[...] = recv[c].astype(F32).reshape(NE * 8, B)
        rows = [stage[pl.ds(r, NE, stride=8), :].astype(BF16) for r in range(8)]
        data = jnp.concatenate(
            [jnp.concatenate(rows[:4], axis=1), jnp.concatenate(rows[4:], axis=1)], axis=0
        )
        return dot(fwd_ref[...], jnp.concatenate([data, data], axis=0))

    wait_swap(g_recv, 0)
    for c in range(3):
        g_spec[c] = spectrum(g_recv, c)
    wait_swap(s_recv, 1)
    for c in range(3):
        spec = spectrum(s_recv, c)
        sr, si = spec[: 2 * NE], spec[2 * NE :]
        gr, gi = g_spec[c, : 2 * NE], g_spec[c, 2 * NE :]
        both = jnp.concatenate([gr * sr - gi * si, gr * si + gi * sr], axis=0)
        upper = both.astype(BF16)
        lower = (both - upper.astype(F32)).astype(BF16)
        sums = dot(back_ref[...], jnp.concatenate([upper, lower, upper], axis=0))
        for r in range(4):
            stage[pl.ds(r, NE, stride=8), :] = sums[:NE, r * B : (r + 1) * B]
            stage[pl.ds(r + 4, NE, stride=8), :] = sums[NE:, r * B : (r + 1) * B]
        c_send[c] = stage[...].reshape(NE, 8, B).astype(BF16)
    swap(c_send, c_recv, 2)
    edges([g_next], [g_prev], "wait_recv")
    wait_swap(c_recv, 2)
    edges(c_nexts, c_prevs, "start")

    def place(packed, row, band):
        re, im = unpack(packed.astype(F32))
        s4[row, band, 0] = re.astype(BF16)
        s4[row, band, 1] = im.astype(BF16)

    for c in range(3):
        place(c_recv[c, pl.ds(0, HALF)], 1, c)
        place(c_recv[c, pl.ds(HALF, HALF)], 2, 2 - c)
    edges(c_nexts, c_prevs, "wait_recv")
    for c in range(3):
        place(c_prev[c], 0, 2 - c)
        place(c_next[c], 3, c)
    for half in range(2):
        bands = sandwich_row(g4, s4, 1 + half)
        for band in range(3):
            out_ref[half, band, 0] = bands[band][:, :B].astype(BF16)
            out_ref[half, band, 1] = bands[band][:, B:].astype(BF16)

    edges([w_next, p_next, g_next, *c_nexts], [w_prev, p_prev, g_prev, *c_prevs], "wait_send")
    wait_sent(g_send, 0)
    wait_sent(s_send, 1)
    wait_sent(c_send, 2)


def local(screening, polarization, propagator):
    fwd, back = tables((3.0 * B / NE) ** 0.5)
    four = pltpu.VMEM((4, 3, 2, B, B), BF16)
    full = pltpu.VMEM((3, NE, 8, B), BF16)
    rim = pltpu.VMEM((3, HALF, 8, B), BF16)
    hbm = pl.BlockSpec(memory_space=pl.ANY)
    vmem = pl.BlockSpec(memory_space=pltpu.VMEM)
    out = pl.pallas_call(
        kernel,
        name="self_energy",
        out_shape=jax.ShapeDtypeStruct((2, 3, 2, B, B), BF16),
        in_specs=[hbm, hbm, hbm, vmem, vmem],
        out_specs=vmem,
        scratch_shapes=[
            four, four, four, four,
            full, full, full, full, full, full, rim, rim,
            pltpu.VMEM((3, 4 * NE, 4 * B), F32),
            pltpu.VMEM((NE * 8, B), F32),
            pltpu.SemaphoreType.DMA((3,)),
            pltpu.SemaphoreType.DMA((12,)),
            pltpu.SemaphoreType.DMA((12,)),
            pltpu.SemaphoreType.DMA((3,)),
            pltpu.SemaphoreType.DMA((3,)),
        ],
        compiler_params=pltpu.CompilerParams(
            collective_id=0, has_side_effects=True, vmem_limit_bytes=48 << 20
        ),
    )(screening[0], polarization[0], propagator[0], jnp.asarray(fwd), jnp.asarray(back))
    return out[None]


def solution(mesh):
    spec = P("energy", "space", None, None, None, None)
    return jax.shard_map(
        local, mesh=mesh, in_specs=(spec, spec, spec), out_specs=spec, check_vma=False
    )
```

time: 127 us -> 64.8 us (0.51)
  Pallas kernels: 0 us -> 59 us
  matrix products: 38.8 us -> 0 us
  starting transfers between devices: 35.8 us -> 0 us
  waiting for transfers between devices: 20.7 us -> 0 us
  blocking collectives: 20.2 us -> 0 us
  other arithmetic: 3.18 us -> 0 us
  local copies, waits for them, and re-layouts: 7.44 us -> 5.56 us
    pallas_call x0 -> x1, Pallas kernels: none -> 59 us  [local(): pl.pallas_call(kernel, name='self_energy', out_shape=jax.ShapeDtypeStruct...]
    dot_general x172 -> x0, matrix products: 38.8 us -> none  [the longest x144 23.9 us: product(): return jnp.einsum(form, lhs, rhs, preferred_element_type=jnp.float32)]
    all_to_all x2 -> x0, starting transfers between devices: 22.6 us -> none  [the longest x1 13.4 us: local(): lax.all_to_all(propa_masked, 'energy', split_axis=4, concat_axis=0, tiled...]
    all_to_all x1 -> x0, blocking collectives: 20.2 us -> none  [local(): lax.all_to_all(sigma_owned, 'energy', split_axis=0, concat_axis=4, tiled=...]
    all_to_all x2 -> x0, waiting for transfers between devices: 13.6 us -> none  [the longest x1 10.5 us: local(): lax.all_to_all(screened, 'energy', split_axis=4, concat_axis=0, tiled=True)]
    ppermute x4 -> x0, starting transfers between devices: 13.2 us -> none  [the longest x2 9.31 us: with_halo(): before = lax.ppermute(last, axis, up)]
    ppermute x4 -> x0, waiting for transfers between devices: 7.13 us -> none  [the longest x2 4.4 us: with_halo(): after = lax.ppermute(leading, axis, down)]
    unnamed x8 -> x11, local copies, waits for them, and re-layouts: 1.05 us -> 5.56 us
  transfers between devices with their start and end apart: 6 -> 0, of which waited for: 4 -> 0; matrix products, arithmetic and copies ran while one was open for 17% -> 0% of each run, Pallas kernels for 0% -> 0%
where the time goes in v1:
time: 64.8 us; the launch traced here: 64.6 us
  Pallas kernels  59 us (91%)
  local copies, waits for them, and re-layouts  5.56 us (9%)
    pallas_call x1, Pallas kernels, local(): pl.pallas_call(kernel, name='self_energy', out_shape=jax.ShapeDtypeStruct...  59 us
    unnamed x11, local copies, waits for them, and re-layouts  5.56 us

profile of v1, /device:TPU:1, one launch (start us, length us, event | category | flops | bytes accessed | tf_op | source)
XLA Modules:
  0.0 64.6 jit_solution(5028413935013598196)
XLA Ops:
  0.0 0.0 copy-start
  0.0 1.0 %copy-done = bf16[1,2,3,2,128,128]{5,4,3,2,1,0:T(8,128)(2,1)S(1)} copy-done((bf16[1,2,3,2,128,128]{5,4,3,2,1,0:T(8,128)(2,1)S(1)}, bf16[1,2,3,2,128,128]{5,4,3,2,1,0:T(8,128)(2,1)}, u32[]{:S(2)}) %copy-start) | copy-done | bytes 393240
  1.0 0.0 copy-start.1
  1.0 1.0 %copy-done.1 = bf16[1,2,3,2,128,128]{5,4,3,2,1,0:T(8,128)(2,1)S(1)} copy-done((bf16[1,2,3,2,128,128]{5,4,3,2,1,0:T(8,128)(2,1)S(1)}, bf16[1,2,3,2,128,128]{5,4,3,2,1,0:T(8,128)(2,1)}, u32[]{:S(2)}) %copy-start.1) | copy-done | bytes 393240
  2.0 0.0 copy-start.2
  2.0 1.0 %copy-done.2 = bf16[1,2,3,2,128,128]{5,4,3,2,1,0:T(8,128)(2,1)S(1)} copy-done((bf16[1,2,3,2,128,128]{5,4,3,2,1,0:T(8,128)(2,1)S(1)}, bf16[1,2,3,2,128,128]{5,4,3,2,1,0:T(8,128)(2,1)}, u32[]{:S(2)}) %copy-start.2) | copy-done | bytes 393240
  3.0 0.0 copy-start.3
  3.0 0.9 %copy-done.3 = bf16[128,768]{1,0:T(8,128)(2,1)S(1)} copy-done((bf16[128,768]{1,0:T(8,128)(2,1)S(1)}, bf16[128,768]{1,0:T(8,128)(2,1)}, u32[]{:S(2)}) %copy-start.3) | copy-done | bytes 196632
  3.9 0.0 copy-start.4
  3.9 0.9 %copy-done.4 = bf16[256,256]{1,0:T(8,128)(2,1)S(1)} copy-done((bf16[256,256]{1,0:T(8,128)(2,1)S(1)}, bf16[256,256]{1,0:T(8,128)(2,1)}, u32[]{:S(2)}) %copy-start.4) | copy-done | bytes 131096
  4.8 59.0 %self_energy.1 = bf16[2,3,2,128,128]{4,3,2,1,0:T(8,128)(2,1)S(1)} custom-call(bf16[2,3,2,128,128]{4,3,2,1,0:T(8,128)(2,1)S(1)} %bitcast.5, bf16[2,3,2,128,128]{4,3,2,1,0:T(8,128)(2,1)S(1)} %bitcast.6, bf16[2,3,2,128,128]{4,3,2,1,0:T(8,128)(2,1)S(1)} %bitcast.7, bf16[256,256]{1,0:T(8,128)(2,1)S(1)} %copy-done.4, bf16[128,768]{1,0:T(8,128)(2,1)S(1)} %copy-done.3), custom_call_target="tpu_custom_call" | custom-call | tf_op jit(solution)/shard_map/self_energy/pallas_call | solution.py:268
  63.9 0.7 %copy.7 = bf16[1,2,3,2,128,128]{5,4,3,2,1,0:T(8,128)(2,1)} copy(bf16[1,2,3,2,128,128]{5,4,3,2,1,0:T(8,128)(2,1)S(1)} %bitcast.4) | data formatting | bytes 786432
Async XLA Ops:
  0.0 1.0 %copy-start = (bf16[1,2,3,2,128,128]{5,4,3,2,1,0:T(8,128)(2,1)S(1)}, bf16[1,2,3,2,128,128]{5,4,3,2,1,0:T(8,128)(2,1)}, u32[]{:S(2)}) copy-start(bf16[1,2,3,2,128,128]{5,4,3,2,1,0:T(8,128)(2,1)} %param.5) | copy-start | bytes 1179652
  1.0 1.0 %copy-start.1 = (bf16[1,2,3,2,128,128]{5,4,3,2,1,0:T(8,128)(2,1)S(1)}, bf16[1,2,3,2,128,128]{5,4,3,2,1,0:T(8,128)(2,1)}, u32[]{:S(2)}) copy-start(bf16[1,2,3,2,128,128]{5,4,3,2,1,0:T(8,128)(2,1)} %param.6) | copy-start | bytes 1179652
  2.0 1.0 %copy-start.2 = (bf16[1,2,3,2,128,128]{5,4,3,2,1,0:T(8,128)(2,1)S(1)}, bf16[1,2,3,2,128,128]{5,4,3,2,1,0:T(8,128)(2,1)}, u32[]{:S(2)}) copy-start(bf16[1,2,3,2,128,128]{5,4,3,2,1,0:T(8,128)(2,1)} %param.7) | copy-start | bytes 1179652
  3.0 0.9 %copy-start.3 = (bf16[128,768]{1,0:T(8,128)(2,1)S(1)}, bf16[128,768]{1,0:T(8,128)(2,1)}, u32[]{:S(2)}) copy-start(bf16[128,768]{1,0:T(8,128)(2,1)} %constant.5.clone.back_ref) | copy-start | bytes 589828
  3.9 0.9 %copy-start.4 = (bf16[256,256]{1,0:T(8,128)(2,1)S(1)}, bf16[256,256]{1,0:T(8,128)(2,1)}, u32[]{:S(2)}) copy-start(bf16[256,256]{1,0:T(8,128)(2,1)} %constant.4.clone.fwd_ref) | copy-start | bytes 393220

commit v2 on v1

v2 whole, which is shorter than its diff:
```python
import math

import jax
import jax.numpy as jnp
import ml_dtypes
import numpy as np
from jax import lax
from jax.experimental import pallas as pl
from jax.experimental.pallas import tpu as pltpu
from jax.sharding import PartitionSpec as P

MESH = pl.DeviceIdType.MESH
B = 128
NE = 64
NS = 4
HALF = NE // 2
F32 = jnp.float32
BF16 = jnp.bfloat16


def split_np(table):
    upper = table.astype(ml_dtypes.bfloat16)
    lower = (table - upper.astype(np.float64)).astype(ml_dtypes.bfloat16)
    return upper, lower


def tables(factor):
    freq = np.arange(2 * NE)
    time = np.arange(NE)
    angle = (freq[:, None] * time[None, :] % (2 * NE)) * (math.pi / NE)
    cos, sin = np.cos(angle), np.sin(angle)
    fwd = np.block([[cos, sin], [-sin, cos]])
    back = np.block([[cos.T, -sin.T], [sin.T, cos.T]]) * (factor / (2 * NE))
    fh, fl = split_np(fwd)
    bh, bl = split_np(back)
    return np.concatenate([fh, fl], 1), np.concatenate([bh, bh, bl], 1)


def dot(a, b):
    return jnp.dot(a, b, preferred_element_type=F32)


def dot_nt(a, b):
    return lax.dot_general(a, b, (((1,), (1,)), ((), ())), preferred_element_type=F32)


def wide(ref, row, band):
    return jnp.concatenate([ref[row, band, 0], ref[row, band, 1]], axis=1)


def embed(ref, row, band):
    re, im = ref[row, band, 0], ref[row, band, 1]
    return jnp.concatenate(
        [jnp.concatenate([re, im], axis=1), jnp.concatenate([-im, re], axis=1)], axis=0
    )


def products_row(outer, inner, row):
    products = {}
    for offset in range(-2, 3):
        steps = [k for k in (-1, 0, 1) if abs(offset - k) <= 1]
        lhs = jnp.concatenate([wide(outer, row, k + 1) for k in steps], axis=1)
        rhs = jnp.concatenate([embed(inner, row + k, offset - k + 1) for k in steps], axis=0)
        products[offset] = dot(lhs, rhs).astype(BF16)
    return products


def close_row(products, outer, row, band):
    offsets = range(band - 2, band + 1)
    lhs = jnp.concatenate([products[d] for d in offsets], axis=1)
    rhs = jnp.concatenate([embed(outer, row + band - 1, d - band + 2) for d in offsets], axis=1)
    return dot_nt(lhs, rhs)


def pack(re, im):
    re, im = re.reshape(16, 8, B), im.reshape(16, 8, B)
    low = lax.broadcasted_iota(jnp.int32, (16, 8, B), 1) < 4
    even = jnp.where(low, re, pltpu.roll(im, 4, 1))
    odd = jnp.where(low, pltpu.roll(re, 4, 1), im)
    return jnp.stack([even, odd], axis=1).reshape(HALF, 8, B)


def unpack(packed):
    pairs = packed.reshape(16, 2, 8, B)
    even, odd = pairs[:, 0], pairs[:, 1]
    low = lax.broadcasted_iota(jnp.int32, (16, 8, B), 1) < 4
    re = jnp.where(low, even, pltpu.roll(odd, 4, 1))
    im = jnp.where(low, pltpu.roll(even, 4, 1), odd)
    return re.reshape(B, B), im.reshape(B, B)


def kernel(
    w_hbm, p_hbm, g_hbm, fwd_hbm, back_hbm, out_ref,
    w4, p4, g4, s4, g_send, g_recv, s_send, s_recv, c_send, c_recv, c_prev, c_next,
    fwd_ref, back_ref, g_spec, stage, load_sem, edge_send, edge_recv, swap_send, swap_recv,
):
    e = lax.axis_index("energy")
    s = lax.axis_index("space")
    barrier = pltpu.get_barrier_semaphore()
    loads = [
        pltpu.make_async_copy(src, dst.at[pl.ds(1, 2)], load_sem.at[i])
        for i, (src, dst) in enumerate(((g_hbm, g4), (w_hbm, w4), (p_hbm, p4)))
    ]
    table_loads = [
        pltpu.make_async_copy(fwd_hbm, fwd_ref, load_sem.at[3]),
        pltpu.make_async_copy(back_hbm, back_ref, load_sem.at[4]),
    ]
    for load in loads + table_loads:
        load.start()

    def greet(i, carry):
        pl.semaphore_signal(barrier, inc=1, device_id=(lax.rem(e + i, NE), s), device_id_type=MESH)
        return carry

    @pl.when(s > 0)
    def _():
        pl.semaphore_signal(barrier, inc=1, device_id=(e, s - 1), device_id_type=MESH)

    @pl.when(s < NS - 1)
    def _():
        pl.semaphore_signal(barrier, inc=1, device_id=(e, s + 1), device_id_type=MESH)

    lax.fori_loop(1, NE, greet, 0)

    first, last = s == 0, s == NS - 1
    low = e < HALF
    idle = (first & low) | (last & jnp.logical_not(low))
    for load in loads:
        load.wait()

    @pl.when(first)
    def _():
        for ref in (w4, p4, g4):
            ref[0] = jnp.zeros(ref.shape[1:], BF16)
            ref[1, 0] = jnp.zeros(ref.shape[2:], BF16)
        c_prev[...] = jnp.zeros(c_prev.shape, BF16)
        c_recv[0, :HALF] = jnp.zeros((HALF, 8, B), BF16)

    @pl.when(last)
    def _():
        for ref in (w4, p4, g4):
            ref[3] = jnp.zeros(ref.shape[1:], BF16)
            ref[2, 2] = jnp.zeros(ref.shape[2:], BF16)
        c_next[...] = jnp.zeros(c_next.shape, BF16)
        c_recv[0, HALF:] = jnp.zeros((HALF, 8, B), BF16)

    pl.semaphore_wait(barrier, NE - 1 + (s > 0).astype(jnp.int32) + (s < NS - 1).astype(jnp.int32))

    def to_next(src, dst, i):
        return pltpu.make_async_remote_copy(
            src, dst, edge_send.at[i], edge_recv.at[i], device_id=(e, s + 1), device_id_type=MESH
        )

    def to_prev(src, dst, i):
        return pltpu.make_async_remote_copy(
            src, dst, edge_send.at[i], edge_recv.at[i], device_id=(e, s - 1), device_id_type=MESH
        )

    groups = (pl.ds(1, 2), pl.ds(0, 1))
    w_next, w_prev = to_next(w4.at[2], w4.at[0], 0), to_prev(w4.at[1], w4.at[3], 1)
    p_next, p_prev = to_next(p4.at[2], p4.at[0], 2), to_prev(p4.at[1], p4.at[3], 3)
    g_next, g_prev = to_next(g4.at[2], g4.at[0], 4), to_prev(g4.at[1], g4.at[3], 5)
    c_nexts = [
        to_next(c_recv.at[part, pl.ds(HALF, HALF)], c_prev.at[part], 6 + k)
        for k, part in enumerate(groups)
    ]
    c_prevs = [
        to_prev(c_recv.at[part, pl.ds(0, HALF)], c_next.at[part], 8 + k)
        for k, part in enumerate(groups)
    ]

    def edges(nexts, prevs, action):
        forward, backward = (prevs, nexts) if action == "wait_recv" else (nexts, prevs)

        @pl.when(s < NS - 1)
        def _():
            for copy in forward:
                getattr(copy, action)()

        @pl.when(s > 0)
        def _():
            for copy in backward:
                getattr(copy, action)()

    def swap(send, recv, slot, k, back=False):
        part = groups[k]

        def body(i, carry):
            to = lax.rem(e + i, NE)
            copy = pltpu.make_async_remote_copy(
                send.at[part, to], recv.at[part, e], swap_send.at[slot], swap_recv.at[slot],
                device_id=(to, s), device_id_type=MESH,
            )
            if k == 0 or back:
                copy.start()
            else:
                nothing = (first & (to < HALF)) | (last & (to >= HALF))

                @pl.when(jnp.logical_not(nothing))
                def _():
                    copy.start()

            return carry

        def run():
            lax.fori_loop(1, NE, body, 0)
            own = pltpu.make_async_copy(send.at[part, e], recv.at[part, e], swap_recv.at[slot])
            own.start()

        if k == 0:
            run()
        elif back:
            pl.when(jnp.logical_not(idle))(run)
        else:
            lax.fori_loop(1, NE, body, 0)

            @pl.when(jnp.logical_not(idle))
            def _():
                pltpu.make_async_copy(
                    send.at[part, e], recv.at[part, e], swap_recv.at[slot]
                ).start()

    def finish(ref, sem, count, k):
        full = ref.at[groups[k], pl.ds(0, count)]
        pltpu.make_async_copy(full, full, sem).wait()

    def wait_swap(recv, slot, k, back=False):
        sem = swap_recv.at[slot]
        if k == 0:
            finish(recv, sem, NE, k)
        elif back:
            ends = first | last
            pl.when(ends)(lambda: finish(recv, sem, HALF, k))
            pl.when(jnp.logical_not(ends))(lambda: finish(recv, sem, NE, k))
        else:
            pl.when(jnp.logical_not(idle))(lambda: finish(recv, sem, NE, k))

    def wait_sent(send, slot, k, back=False):
        sem = swap_send.at[slot]
        if k == 0:
            finish(send, sem, NE - 1, k)
        elif back:
            pl.when(jnp.logical_not(idle))(lambda: finish(send, sem, NE - 1, k))
        else:
            ends = first | last
            pl.when(jnp.logical_not(ends))(lambda: finish(send, sem, NE - 1, k))
            pl.when(idle)(lambda: finish(send, sem, HALF, k))
            pl.when(ends & jnp.logical_not(idle))(lambda: finish(send, sem, HALF - 1, k))

    members = ((1, 2), (0,))
    edges([w_next, p_next], [w_prev, p_prev], "start")
    for k in range(2):
        for c in members[k]:
            for half in range(2):
                band = c if half == 0 else 2 - c
                re = g4[1 + half, band, 0].astype(F32)
                im = g4[1 + half, band, 1].astype(F32)
                g_send[c, pl.ds(half * HALF, HALF)] = pack(re, im).astype(BF16)
        swap(g_send, g_recv, k, k)

    @pl.when(idle)
    def _():
        g_recv[0] = jnp.zeros(g_recv.shape[1:], BF16)
        s_recv[0] = jnp.zeros(s_recv.shape[1:], BF16)

    edges([w_next, p_next], [w_prev, p_prev], "wait_recv")
    firsts = [products_row(w4, p4, 1 + half) for half in range(2)]
    for k in range(2):
        for c in members[k]:
            for half in range(2):
                band = c if half == 0 else 2 - c
                block = close_row(firsts[half], w4, 1 + half, band)
                s_send[c, pl.ds(half * HALF, HALF)] = pack(block[:, :B], block[:, B:]).astype(BF16)
        swap(s_send, s_recv, 2 + k, k)
    edges([g_next], [g_prev], "start")

    def spectrum(recv, c):
        stage[...] = recv[c].astype(F32).reshape(NE * 8, B)
        rows = [stage[pl.ds(r, NE, stride=8), :].astype(BF16) for r in range(8)]
        data = jnp.concatenate(
            [jnp.concatenate(rows[:4], axis=1), jnp.concatenate(rows[4:], axis=1)], axis=0
        )
        return dot(fwd_ref[...], jnp.concatenate([data, data], axis=0))

    for load in table_loads:
        load.wait()
    for k in range(2):
        wait_swap(g_recv, k, k)
        for c in members[k]:
            g_spec[c] = spectrum(g_recv, c)
    for k in range(2):
        wait_swap(s_recv, 2 + k, k)
        for c in members[k]:
            spec = spectrum(s_recv, c)
            sr, si = spec[: 2 * NE], spec[2 * NE :]
            gr, gi = g_spec[c, : 2 * NE], g_spec[c, 2 * NE :]
            both = jnp.concatenate([gr * sr - gi * si, gr * si + gi * sr], axis=0)
            upper = both.astype(BF16)
            lower = (both - upper.astype(F32)).astype(BF16)
            sums = dot(back_ref[...], jnp.concatenate([upper, lower, upper], axis=0))
            for r in range(4):
                stage[pl.ds(r, NE, stride=8), :] = sums[:NE, r * B : (r + 1) * B]
                stage[pl.ds(r + 4, NE, stride=8), :] = sums[NE:, r * B : (r + 1) * B]
            c_send[c] = stage[...].reshape(NE, 8, B).astype(BF16)
        swap(c_send, c_recv, 4 + k, k, back=True)
    edges([g_next], [g_prev], "wait_recv")

    def place(packed, row, band):
        re, im = unpack(packed.astype(F32))
        s4[row, band, 0] = re.astype(BF16)
        s4[row, band, 1] = im.astype(BF16)

    for k in range(2):
        wait_swap(c_recv, 4 + k, k, back=True)
        edges(c_nexts[k : k + 1], c_prevs[k : k + 1], "start")
        for c in members[k]:
            place(c_recv[c, pl.ds(0, HALF)], 1, c)
            place(c_recv[c, pl.ds(HALF, HALF)], 2, 2 - c)
    for k in range(2):
        edges(c_nexts[k : k + 1], c_prevs[k : k + 1], "wait_recv")
        for c in members[k]:
            place(c_prev[c], 0, 2 - c)
            place(c_next[c], 3, c)
    for half in range(2):
        products = products_row(g4, s4, 1 + half)
        for band in range(3):
            block = close_row(products, g4, 1 + half, band)
            out_ref[half, band, 0] = block[:, :B].astype(BF16)
            out_ref[half, band, 1] = block[:, B:].astype(BF16)

    edges([w_next, p_next, g_next, *c_nexts], [w_prev, p_prev, g_prev, *c_prevs], "wait_send")
    for k in range(2):
        wait_sent(g_send, k, k)
        wait_sent(s_send, 2 + k, k)
        wait_sent(c_send, 4 + k, k, back=True)


def local(screening, polarization, propagator):
    fwd, back = tables((3.0 * B / NE) ** 0.5)
    four = pltpu.VMEM((4, 3, 2, B, B), BF16)
    full = pltpu.VMEM((3, NE, 8, B), BF16)
    rim = pltpu.VMEM((3, HALF, 8, B), BF16)
    hbm = pl.BlockSpec(memory_space=pltpu.HBM)
    vmem = pl.BlockSpec(memory_space=pltpu.VMEM)
    out = pl.pallas_call(
        kernel,
        name="self_energy",
        out_shape=jax.ShapeDtypeStruct((2, 3, 2, B, B), BF16),
        in_specs=[hbm, hbm, hbm, hbm, hbm],
        out_specs=vmem,
        scratch_shapes=[
            four, four, four, four,
            full, full, full, full, full, full, rim, rim,
            pltpu.VMEM(fwd.shape, BF16),
            pltpu.VMEM(back.shape, BF16),
            pltpu.VMEM((3, 4 * NE, 4 * B), F32),
            pltpu.VMEM((NE * 8, B), F32),
            pltpu.SemaphoreType.DMA((5,)),
            pltpu.SemaphoreType.DMA((10,)),
            pltpu.SemaphoreType.DMA((10,)),
            pltpu.SemaphoreType.DMA((6,)),
            pltpu.SemaphoreType.DMA((6,)),
        ],
        compiler_params=pltpu.CompilerParams(
            collective_id=0, has_side_effects=True, vmem_limit_bytes=62 << 20
        ),
    )(screening[0], polarization[0], propagator[0], jnp.asarray(fwd), jnp.asarray(back))
    return out[None]


def solution(mesh):
    spec = P("energy", "space", None, None, None, None)
    return jax.shard_map(
        local, mesh=mesh, in_specs=(spec, spec, spec), out_specs=spec, check_vma=False
    )
```

time: 64.8 us -> 57.6 us (0.89)
  local copies, waits for them, and re-layouts: 5.56 us -> 1.77 us
  Pallas kernels: 59 us -> 55.7 us
    unnamed x11 -> x1, local copies, waits for them, and re-layouts: 5.56 us -> 1.77 us
    pallas_call x1, Pallas kernels: 59 us -> 55.7 us  [local(): pl.pallas_call(kernel, name='self_energy', out_shape=jax.ShapeDtypeStruct...]
where the time goes in v2:
time: 57.6 us; the launch traced here: 57.5 us
  Pallas kernels  55.7 us (97%)
  local copies, waits for them, and re-layouts  1.77 us (3%)
    pallas_call x1, Pallas kernels, local(): pl.pallas_call(kernel, name='self_energy', out_shape=jax.ShapeDtypeStruct...  55.7 us
    unnamed x1, local copies, waits for them, and re-layouts  1.77 us

profile of v2, /device:TPU:1, one launch (start us, length us, event | category | flops | bytes accessed | tf_op | source)
XLA Modules:
  0.0 57.5 jit_solution(13325435847830825862)
XLA Ops:
  0.0 55.7 %self_energy.1 = bf16[2,3,2,128,128]{4,3,2,1,0:T(8,128)(2,1)} custom-call(bf16[2,3,2,128,128]{4,3,2,1,0:T(8,128)(2,1)} %bitcast.5, bf16[2,3,2,128,128]{4,3,2,1,0:T(8,128)(2,1)} %bitcast.6, bf16[2,3,2,128,128]{4,3,2,1,0:T(8,128)(2,1)} %bitcast.7, bf16[256,256]{1,0:T(8,128)(2,1)} %constant.4.clone.fwd_hbm, bf16[128,768]{1,0:T(8,128)(2,1)} %constant.5.clone.back_hbm), custom_call_target="tpu_custom_call" | custom-call | tf_op jit(solution)/shard_map/self_energy/pallas_call | solution.py:345
  55.7 1.8 %copy.7 = bf16[1,2,3,2,128,128]{5,4,3,2,1,0:T(8,128)(2,1)} copy(bf16[1,2,3,2,128,128]{5,4,3,2,1,0:T(8,128)(2,1)} %bitcast.4) | data formatting | bytes 786432

commit v3 on v2

--- a/solution.py
+++ b/solution.py
@@ -220,6 +220,58 @@
                     send.at[part, e], recv.at[part, e], swap_recv.at[slot]
                 ).start()
 
+    def swap_all(send, recv, slot):
+        def copy(part, to):
+            return pltpu.make_async_remote_copy(
+                send.at[part, to], recv.at[part, e], swap_send.at[slot], swap_recv.at[slot],
+                device_id=(to, s), device_id_type=MESH,
+            )
+
+        def body(i, carry):
+            to = lax.rem(e + i, NE)
+            nothing = (first & (to < HALF)) | (last & (to >= HALF))
+
+            @pl.when(nothing)
+            def _():
+                copy(pl.ds(1, 2), to).start()
+
+            @pl.when(jnp.logical_not(nothing))
+            def _():
+                copy(pl.ds(0, 3), to).start()
+
+            return carry
+
+        lax.fori_loop(1, NE, body, 0)
+
+        @pl.when(idle)
+        def _():
+            own = pl.ds(1, 2)
+            pltpu.make_async_copy(send.at[own, e], recv.at[own, e], swap_recv.at[slot]).start()
+
+        @pl.when(jnp.logical_not(idle))
+        def _():
+            pltpu.make_async_copy(send.at[:, e], recv.at[:, e], swap_recv.at[slot]).start()
+
+    def wait_all(recv, slot):
+        sem = swap_recv.at[slot]
+
+        @pl.when(idle)
+        def _():
+            pltpu.make_async_copy(recv.at[pl.ds(1, 2)], recv.at[pl.ds(1, 2)], sem).wait()
+
+        @pl.when(jnp.logical_not(idle))
+        def _():
+            pltpu.make_async_copy(recv, recv, sem).wait()
+
+    def wait_all_sent(send, slot):
+        sem = swap_send.at[slot]
+        pair = send.at[pl.ds(1, 2), pl.ds(0, NE - 1)]
+        pltpu.make_async_copy(pair, pair, sem).wait()
+        ends = first | last
+        pl.when(jnp.logical_not(ends))(lambda: finish(send, sem, NE - 1, 1))
+        pl.when(idle)(lambda: finish(send, sem, HALF, 1))
+        pl.when(ends & jnp.logical_not(idle))(lambda: finish(send, sem, HALF - 1, 1))
+
     def finish(ref, sem, count, k):
         full = ref.at[groups[k], pl.ds(0, count)]
         pltpu.make_async_copy(full, full, sem).wait()
@@ -249,14 +301,16 @@
 
     members = ((1, 2), (0,))
     edges([w_next, p_next], [w_prev, p_prev], "start")
-    for k in range(2):
-        for c in members[k]:
-            for half in range(2):
-                band = c if half == 0 else 2 - c
-                re = g4[1 + half, band, 0].astype(F32)
-                im = g4[1 + half, band, 1].astype(F32)
-                g_send[c, pl.ds(half * HALF, HALF)] = pack(re, im).astype(BF16)
-        swap(g_send, g_recv, k, k)
+    for c in range(3):
+        for half in range(2):
+            band = c if half == 0 else 2 - c
+            re = g4[1 + half, band, 0].astype(F32)
+            im = g4[1 + half, band, 1].astype(F32)
+            g_send[c, pl.ds(half * HALF, HALF)] = pack(re, im).astype(BF16)
+    @pl.when(jnp.logical_not(first | last))
+    def _():
+        swap_all(g_send, g_recv, 0)
+
 
     @pl.when(idle)
     def _():
@@ -272,6 +326,10 @@
                 block = close_row(firsts[half], w4, 1 + half, band)
                 s_send[c, pl.ds(half * HALF, HALF)] = pack(block[:, :B], block[:, B:]).astype(BF16)
         swap(s_send, s_recv, 2 + k, k)
+    @pl.when(first | last)
+    def _():
+        swap_all(g_send, g_recv, 0)
+
     edges([g_next], [g_prev], "start")
 
     def spectrum(recv, c):
@@ -284,10 +342,9 @@
 
     for load in table_loads:
         load.wait()
-    for k in range(2):
-        wait_swap(g_recv, k, k)
-        for c in members[k]:
-            g_spec[c] = spectrum(g_recv, c)
+    wait_all(g_recv, 0)
+    for c in range(3):
+        g_spec[c] = spectrum(g_recv, c)
     for k in range(2):
         wait_swap(s_recv, 2 + k, k)
         for c in members[k]:
@@ -329,8 +386,8 @@
             out_ref[half, band, 1] = block[:, B:].astype(BF16)
 
     edges([w_next, p_next, g_next, *c_nexts], [w_prev, p_prev, g_prev, *c_prevs], "wait_send")
+    wait_all_sent(g_send, 0)
     for k in range(2):
-        wait_sent(g_send, k, k)
         wait_sent(s_send, 2 + k, k)
         wait_sent(c_send, 4 + k, k, back=True)
 

time: 57.6 us -> 55.7 us (0.967)
  Pallas kernels: 55.7 us -> 53.8 us
    pallas_call x1, Pallas kernels: 55.7 us -> 53.8 us  [local(): pl.pallas_call(kernel, name='self_energy', out_shape=jax.ShapeDtypeStruct...]
where the time goes in v3:
time: 55.7 us; the launch traced here: 55.6 us
  Pallas kernels  53.8 us (97%)
  local copies, waits for them, and re-layouts  1.77 us (3%)
    pallas_call x1, Pallas kernels, local(): pl.pallas_call(kernel, name='self_energy', out_shape=jax.ShapeDtypeStruct...  53.8 us
    unnamed x1, local copies, waits for them, and re-layouts  1.77 us

profile of v3, /device:TPU:1, one launch (start us, length us, event | category | flops | bytes accessed | tf_op | source)
XLA Modules:
  0.0 55.6 jit_solution(14097327660846934014)
XLA Ops:
  0.0 53.8 %self_energy.1 = bf16[2,3,2,128,128]{4,3,2,1,0:T(8,128)(2,1)} custom-call(bf16[2,3,2,128,128]{4,3,2,1,0:T(8,128)(2,1)} %bitcast.5, bf16[2,3,2,128,128]{4,3,2,1,0:T(8,128)(2,1)} %bitcast.6, bf16[2,3,2,128,128]{4,3,2,1,0:T(8,128)(2,1)} %bitcast.7, bf16[256,256]{1,0:T(8,128)(2,1)} %constant.4.clone.fwd_hbm, bf16[128,768]{1,0:T(8,128)(2,1)} %constant.5.clone.back_hbm), custom_call_target="tpu_custom_call" | custom-call | tf_op jit(solution)/shard_map/self_energy/pallas_call | solution.py:402
  53.8 1.8 %copy.7 = bf16[1,2,3,2,128,128]{5,4,3,2,1,0:T(8,128)(2,1)} copy(bf16[1,2,3,2,128,128]{5,4,3,2,1,0:T(8,128)(2,1)} %bitcast.4) | data formatting | bytes 786432

commit v4 on v3

--- a/solution.py
+++ b/solution.py
@@ -33,7 +33,9 @@
     back = np.block([[cos.T, -sin.T], [sin.T, cos.T]]) * (factor / (2 * NE))
     fh, fl = split_np(fwd)
     bh, bl = split_np(back)
-    return np.concatenate([fh, fl], 1), np.concatenate([bh, bh, bl], 1)
+    table = np.zeros((8 * B, 2 * B), ml_dtypes.bfloat16)
+    table[: 5 * B] = np.concatenate([np.concatenate([fh, fl], 1), bh, bh, bl], 0)
+    return table
 
 
 def dot(a, b):
@@ -90,9 +92,9 @@
 
 
 def kernel(
-    w_hbm, p_hbm, g_hbm, fwd_hbm, back_hbm, out_ref,
+    w_hbm, p_hbm, g_hbm, table_hbm, out_ref,
     w4, p4, g4, s4, g_send, g_recv, s_send, s_recv, c_send, c_recv, c_prev, c_next,
-    fwd_ref, back_ref, g_spec, stage, load_sem, edge_send, edge_recv, swap_send, swap_recv,
+    table, g_spec, stage, load_sem, edge_send, edge_recv, swap_send, swap_recv,
 ):
     e = lax.axis_index("energy")
     s = lax.axis_index("space")
@@ -102,8 +104,7 @@
         for i, (src, dst) in enumerate(((g_hbm, g4), (w_hbm, w4), (p_hbm, p4)))
     ]
     table_loads = [
-        pltpu.make_async_copy(fwd_hbm, fwd_ref, load_sem.at[3]),
-        pltpu.make_async_copy(back_hbm, back_ref, load_sem.at[4]),
+        pltpu.make_async_copy(table_hbm.at[pl.ds(0, 5 * B)], table, load_sem.at[3]),
     ]
     for load in loads + table_loads:
         load.start()
@@ -338,7 +339,7 @@
         data = jnp.concatenate(
             [jnp.concatenate(rows[:4], axis=1), jnp.concatenate(rows[4:], axis=1)], axis=0
         )
-        return dot(fwd_ref[...], jnp.concatenate([data, data], axis=0))
+        return dot(table[: 2 * B], jnp.concatenate([data, data], axis=0))
 
     for load in table_loads:
         load.wait()
@@ -354,7 +355,8 @@
             both = jnp.concatenate([gr * sr - gi * si, gr * si + gi * sr], axis=0)
             upper = both.astype(BF16)
             lower = (both - upper.astype(F32)).astype(BF16)
-            sums = dot(back_ref[...], jnp.concatenate([upper, lower, upper], axis=0))
+            back = jnp.concatenate([table[k * B : (k + 1) * B] for k in (2, 3, 4)], axis=1)
+            sums = dot(back, jnp.concatenate([upper, lower, upper], axis=0))
             for r in range(4):
                 stage[pl.ds(r, NE, stride=8), :] = sums[:NE, r * B : (r + 1) * B]
                 stage[pl.ds(r + 4, NE, stride=8), :] = sums[NE:, r * B : (r + 1) * B]
@@ -393,7 +395,7 @@
 
 
 def local(screening, polarization, propagator):
-    fwd, back = tables((3.0 * B / NE) ** 0.5)
+    table = tables((3.0 * B / NE) ** 0.5)
     four = pltpu.VMEM((4, 3, 2, B, B), BF16)
     full = pltpu.VMEM((3, NE, 8, B), BF16)
     rim = pltpu.VMEM((3, HALF, 8, B), BF16)
@@ -403,25 +405,24 @@
         kernel,
         name="self_energy",
         out_shape=jax.ShapeDtypeStruct((2, 3, 2, B, B), BF16),
-        in_specs=[hbm, hbm, hbm, hbm, hbm],
+        in_specs=[hbm, hbm, hbm, hbm],
         out_specs=vmem,
         scratch_shapes=[
             four, four, four, four,
             full, full, full, full, full, full, rim, rim,
-            pltpu.VMEM(fwd.shape, BF16),
-            pltpu.VMEM(back.shape, BF16),
+            pltpu.VMEM((5 * B, 2 * B), BF16),
             pltpu.VMEM((3, 4 * NE, 4 * B), F32),
             pltpu.VMEM((NE * 8, B), F32),
-            pltpu.SemaphoreType.DMA((5,)),
+            pltpu.SemaphoreType.DMA((4,)),
             pltpu.SemaphoreType.DMA((10,)),
             pltpu.SemaphoreType.DMA((10,)),
             pltpu.SemaphoreType.DMA((6,)),
             pltpu.SemaphoreType.DMA((6,)),
         ],
         compiler_params=pltpu.CompilerParams(
-            collective_id=0, has_side_effects=True, vmem_limit_bytes=62 << 20
+            collective_id=0, has_side_effects=True, vmem_limit_bytes=54848 << 10
         ),
-    )(screening[0], polarization[0], propagator[0], jnp.asarray(fwd), jnp.asarray(back))
+    )(screening[0], polarization[0], propagator[0], jnp.asarray(table))
     return out[None]
 
 

time: 55.7 us -> 54 us (0.969)
  local copies, waits for them, and re-layouts: 1.77 us -> 0.75 us
  Pallas kernels: 53.8 us -> 53.1 us
    unnamed x1, local copies, waits for them, and re-layouts: 1.77 us -> 0.75 us
    pallas_call x1, Pallas kernels: 53.8 us -> 53.1 us  [local(): pl.pallas_call(kernel, name='self_energy', out_shape=jax.ShapeDtypeStruct...]
where the time goes in v4:
time: 54 us; the launch traced here: 53.9 us
  Pallas kernels  53.1 us (98%)
  local copies, waits for them, and re-layouts  0.75 us (1%)
    pallas_call x1, Pallas kernels, local(): pl.pallas_call(kernel, name='self_energy', out_shape=jax.ShapeDtypeStruct...  53.1 us

profile of v4, /device:TPU:1, one launch (start us, length us, event | category | flops | bytes accessed | tf_op | source)
XLA Modules:
  0.0 53.9 jit_solution(3692648448995981788)
XLA Ops:
  0.0 53.1 %self_energy.1 = bf16[2,3,2,128,128]{4,3,2,1,0:T(8,128)(2,1)S(1)} custom-call(bf16[2,3,2,128,128]{4,3,2,1,0:T(8,128)(2,1)} %bitcast.5, bf16[2,3,2,128,128]{4,3,2,1,0:T(8,128)(2,1)} %bitcast.6, bf16[2,3,2,128,128]{4,3,2,1,0:T(8,128)(2,1)} %bitcast.7, bf16[1024,256]{1,0:T(8,128)(2,1)} %constant.2.clone.table_hbm), custom_call_target="tpu_custom_call" | custom-call | tf_op jit(solution)/shard_map/self_energy/pallas_call | solution.py:404
  53.1 0.7 %copy.6 = bf16[1,2,3,2,128,128]{5,4,3,2,1,0:T(8,128)(2,1)} copy(bf16[1,2,3,2,128,128]{5,4,3,2,1,0:T(8,128)(2,1)S(1)} %bitcast.4) | data formatting | bytes 786432

commit v5 on v4

--- a/solution.py
+++ b/solution.py
@@ -375,17 +375,38 @@
         for c in members[k]:
             place(c_recv[c, pl.ds(0, HALF)], 1, c)
             place(c_recv[c, pl.ds(HALF, HALF)], 2, 2 - c)
-    for k in range(2):
-        edges(c_nexts[k : k + 1], c_prevs[k : k + 1], "wait_recv")
-        for c in members[k]:
+    def take_prev():
+        @pl.when(s > 0)
+        def _():
+            for copy in c_nexts:
+                copy.wait_recv()
+
+        for c in range(3):
             place(c_prev[c], 0, 2 - c)
+
+    def take_next():
+        @pl.when(s < NS - 1)
+        def _():
+            for copy in c_prevs:
+                copy.wait_recv()
+
+        for c in range(3):
             place(c_next[c], 3, c)
-    for half in range(2):
+
+    def dress(half):
         products = products_row(g4, s4, 1 + half)
         for band in range(3):
             block = close_row(products, g4, 1 + half, band)
             out_ref[half, band, 0] = block[:, :B].astype(BF16)
             out_ref[half, band, 1] = block[:, B:].astype(BF16)
+
+    near = (s >= NS // 2).astype(jnp.int32)
+    pl.when(near == 0)(take_prev)
+    pl.when(near == 1)(take_next)
+    dress(near)
+    pl.when(near == 0)(take_next)
+    pl.when(near == 1)(take_prev)
+    dress(1 - near)
 
     edges([w_next, p_next, g_next, *c_nexts], [w_prev, p_prev, g_prev, *c_prevs], "wait_send")
     wait_all_sent(g_send, 0)

time: 54 us -> 53.6 us (level)
  no operation moved by 1% of the time
where the time goes in v5:
time: 53.6 us; the launch traced here: 53.5 us
  Pallas kernels  52.8 us (99%)
  local copies, waits for them, and re-layouts  0.75 us (1%)
    pallas_call x1, Pallas kernels, local(): pl.pallas_call(kernel, name='self_energy', out_shape=jax.ShapeDtypeStruct...  52.8 us

profile of v5, /device:TPU:1, one launch (start us, length us, event | category | flops | bytes accessed | tf_op | source)
XLA Modules:
  0.0 53.5 jit_solution(5130756649754178758)
XLA Ops:
  0.0 52.8 %self_energy.1 = bf16[2,3,2,128,128]{4,3,2,1,0:T(8,128)(2,1)S(1)} custom-call(bf16[2,3,2,128,128]{4,3,2,1,0:T(8,128)(2,1)} %bitcast.5, bf16[2,3,2,128,128]{4,3,2,1,0:T(8,128)(2,1)} %bitcast.6, bf16[2,3,2,128,128]{4,3,2,1,0:T(8,128)(2,1)} %bitcast.7, bf16[1024,256]{1,0:T(8,128)(2,1)} %constant.2.clone.table_hbm), custom_call_target="tpu_custom_call" | custom-call | tf_op jit(solution)/shard_map/self_energy/pallas_call | solution.py:425
  52.8 0.7 %copy.6 = bf16[1,2,3,2,128,128]{5,4,3,2,1,0:T(8,128)(2,1)} copy(bf16[1,2,3,2,128,128]{5,4,3,2,1,0:T(8,128)(2,1)S(1)} %bitcast.4) | data formatting | bytes 786432

commit v6 on v5

--- a/solution.py
+++ b/solution.py
@@ -106,9 +106,6 @@
     table_loads = [
         pltpu.make_async_copy(table_hbm.at[pl.ds(0, 5 * B)], table, load_sem.at[3]),
     ]
-    for load in loads + table_loads:
-        load.start()
-
     def greet(i, carry):
         pl.semaphore_signal(barrier, inc=1, device_id=(lax.rem(e + i, NE), s), device_id_type=MESH)
         return carry
@@ -122,29 +119,12 @@
         pl.semaphore_signal(barrier, inc=1, device_id=(e, s + 1), device_id_type=MESH)
 
     lax.fori_loop(1, NE, greet, 0)
+    for load in loads + table_loads:
+        load.start()
 
     first, last = s == 0, s == NS - 1
     low = e < HALF
     idle = (first & low) | (last & jnp.logical_not(low))
-    for load in loads:
-        load.wait()
-
-    @pl.when(first)
-    def _():
-        for ref in (w4, p4, g4):
-            ref[0] = jnp.zeros(ref.shape[1:], BF16)
-            ref[1, 0] = jnp.zeros(ref.shape[2:], BF16)
-        c_prev[...] = jnp.zeros(c_prev.shape, BF16)
-        c_recv[0, :HALF] = jnp.zeros((HALF, 8, B), BF16)
-
-    @pl.when(last)
-    def _():
-        for ref in (w4, p4, g4):
-            ref[3] = jnp.zeros(ref.shape[1:], BF16)
-            ref[2, 2] = jnp.zeros(ref.shape[2:], BF16)
-        c_next[...] = jnp.zeros(c_next.shape, BF16)
-        c_recv[0, HALF:] = jnp.zeros((HALF, 8, B), BF16)
-
     pl.semaphore_wait(barrier, NE - 1 + (s > 0).astype(jnp.int32) + (s < NS - 1).astype(jnp.int32))
 
     def to_next(src, dst, i):
@@ -158,8 +138,8 @@
         )
 
     groups = (pl.ds(1, 2), pl.ds(0, 1))
-    w_next, w_prev = to_next(w4.at[2], w4.at[0], 0), to_prev(w4.at[1], w4.at[3], 1)
-    p_next, p_prev = to_next(p4.at[2], p4.at[0], 2), to_prev(p4.at[1], p4.at[3], 3)
+    w_next, w_prev = to_next(w_hbm.at[1], w4.at[0], 0), to_prev(w_hbm.at[0], w4.at[3], 1)
+    p_next, p_prev = to_next(p_hbm.at[1], p4.at[0], 2), to_prev(p_hbm.at[0], p4.at[3], 3)
     g_next, g_prev = to_next(g4.at[2], g4.at[0], 4), to_prev(g4.at[1], g4.at[3], 5)
     c_nexts = [
         to_next(c_recv.at[part, pl.ds(HALF, HALF)], c_prev.at[part], 6 + k)
@@ -302,6 +282,25 @@
 
     members = ((1, 2), (0,))
     edges([w_next, p_next], [w_prev, p_prev], "start")
+    for load in loads:
+        load.wait()
+
+    @pl.when(first)
+    def _():
+        for ref in (w4, p4, g4):
+            ref[0] = jnp.zeros(ref.shape[1:], BF16)
+            ref[1, 0] = jnp.zeros(ref.shape[2:], BF16)
+        c_prev[...] = jnp.zeros(c_prev.shape, BF16)
+        c_recv[0, :HALF] = jnp.zeros((HALF, 8, B), BF16)
+
+    @pl.when(last)
+    def _():
+        for ref in (w4, p4, g4):
+            ref[3] = jnp.zeros(ref.shape[1:], BF16)
+            ref[2, 2] = jnp.zeros(ref.shape[2:], BF16)
+        c_next[...] = jnp.zeros(c_next.shape, BF16)
+        c_recv[0, HALF:] = jnp.zeros((HALF, 8, B), BF16)
+
     for c in range(3):
         for half in range(2):
             band = c if half == 0 else 2 - c

time: 53.6 us -> 53.6 us (level)
  no operation moved by 1% of the time
where the time goes in v6:
time: 53.6 us; the launch traced here: 53.5 us
  Pallas kernels  52.7 us (98%)
  local copies, waits for them, and re-layouts  0.75 us (1%)
    pallas_call x1, Pallas kernels, local(): pl.pallas_call(kernel, name='self_energy', out_shape=jax.ShapeDtypeStruct...  52.7 us

profile of v6, /device:TPU:1, one launch (start us, length us, event | category | flops | bytes accessed | tf_op | source)
XLA Modules:
  0.0 53.5 jit_solution(17773951819302492470)
XLA Ops:
  0.0 52.7 %self_energy.1 = bf16[2,3,2,128,128]{4,3,2,1,0:T(8,128)(2,1)S(1)} custom-call(bf16[2,3,2,128,128]{4,3,2,1,0:T(8,128)(2,1)} %bitcast.5, bf16[2,3,2,128,128]{4,3,2,1,0:T(8,128)(2,1)} %bitcast.6, bf16[2,3,2,128,128]{4,3,2,1,0:T(8,128)(2,1)} %bitcast.7, bf16[1024,256]{1,0:T(8,128)(2,1)} %constant.2.clone.table_hbm), custom_call_target="tpu_custom_call" | custom-call | tf_op jit(solution)/shard_map/self_energy/pallas_call | solution.py:424
  52.8 0.7 %copy.6 = bf16[1,2,3,2,128,128]{5,4,3,2,1,0:T(8,128)(2,1)} copy(bf16[1,2,3,2,128,128]{5,4,3,2,1,0:T(8,128)(2,1)S(1)} %bitcast.4) | data formatting | bytes 786432
